TPU v7x, 32 devices: a whole 2x2x4 slice. The times are simulated.
32 devices in a mesh: groups: 2 (over x), blk: 16 (over z, y, core).
Axes of the slice: x: 2, y: 2, z: 4, core: 2. Of those that a mesh axis runs over, the one named last changes fastest.
Arguments:
- query_grads: bfloat16 [3584, 65536], P(('groups', 'blk')), parts along dimension 0, may hold values from -6 to 6
- train_grads: bfloat16 [256, 65536], P(('groups', 'blk')), parts along dimension 0, may hold values from -6 to 6
- basis_out: bfloat16 [256, 256], replicated, may hold values from -0.375 to 0.375
- basis_in: bfloat16 [256, 256], replicated, may hold values from -0.375 to 0.375
- eigen_out: float32 [256], replicated, may hold values from 0.3 to 3
- eigen_in: float32 [256], replicated, may hold values from 0.3 to 3
Outputs:
- influence: float32 [3584, 128], P(('groups', 'blk')), parts along dimension 0
- train_totals: float32 [256], P(('groups', 'blk')), parts along dimension 0
There are 2 independent parts, one for each index of `groups`. A program takes and returns all parts, laid end to end along the dimension named above; an argument that names none is the same for every part. Nothing has to cross between parts.
All inputs are finite; a program needn't handle non-finite values.
Results may differ from a plain program's by a relative error of at most 0.0041.
Values may be sent and summed in bfloat16 or wider, within the bound.
A program may use at most 192 MiB of HBM per device.

v0:
```python
import math

import jax
import jax.numpy as jnp
from jax import lax
from jax.sharding import PartitionSpec as P

damping = 0.1


def rotate(gradients, basis_out, basis_in, weights):
    count = gradients.shape[0]
    side = basis_in.shape[0]
    half = jnp.dot(
        gradients.reshape(count * side, side), basis_in, preferred_element_type=jnp.float32
    ).astype(jnp.bfloat16)
    half = half.reshape(count, side, side)
    turned = jnp.einsum("ai,naj->nij", basis_out, half, preferred_element_type=jnp.float32)
    if weights is not None:
        turned = turned * weights
    return turned.astype(jnp.bfloat16).reshape(count, side * side)


def local(query_grads, train_grads, basis_out, basis_in, eigen_out, eigen_in):
    side = basis_in.shape[0]
    local_train = train_grads.shape[0]
    local_query = query_grads.shape[0]
    devices = lax.axis_size("blk")
    weights = 1.0 / (eigen_out[:, None] * eigen_in[None, :] + damping)
    query_eigen = rotate(query_grads, basis_out, basis_in, weights)
    train_eigen = rotate(train_grads, basis_out, basis_in, None)
    raw = lax.dot_general(
        query_eigen,
        lax.all_gather(train_eigen, "blk", axis=0, tiled=True),
        (((1,), (1,)), ((), ())),
        preferred_element_type=jnp.float32,
    )
    influence = raw / float(side)
    column_terms = jnp.sum(influence, axis=0)
    scale = 1.0 / math.sqrt(local_query * devices)
    summed = lax.psum(column_terms, "blk")
    offset = lax.axis_index("blk") * local_train
    mine = lax.dynamic_slice_in_dim(summed, offset, local_train)
    return (influence, mine * scale)


def solution(mesh):
    return jax.shard_map(
        local,
        mesh=mesh,
        in_specs=(P(("groups", "blk"), None), P(("groups", "blk"), None), P(), P(), P(), P()),
        out_specs=(P(("groups", "blk"), None), P(("groups", "blk"))),
        check_vma=False,
    )
```

profile of v0, /device:TPU:0, one launch (start us, length us, event | category | flops | bytes accessed | tf_op | source)
XLA Modules:
  0.0 193.7 jit_solution(16862624950374742318)
XLA Ops:
  7.2 0.0 copy-start
  7.2 0.0 all-gather.2.cloned.1.call-start
  7.2 1.7 reshape.54
  9.0 0.0 copy-done
  9.0 0.4 convolution_convert_fusion.1
  9.4 1.4 fusion.1
  10.8 0.5 copy.13
  11.3 1.6 copy.17
  12.9 0.0 all-gather.2.cloned.1.call-update
  12.9 0.0 copy-start.3
  12.9 0.0 copy-start.4
  12.9 18.1 %reshape.51 = bf16[28672,256]{1,0:T(8,128)(2,1)} reshape(bf16[112,65536]{1,0:T(8,128)(2,1)} %param.6) | data formatting | bytes 29360128 | tf_op jit(solution)/shard_map/reshape | solution.py:15
  31.0 0.0 copy-done.3
  31.0 0.0 copy-done.4
  31.0 0.1 add_divide_fusion
  31.1 0.0 copy-start.2
  31.1 14.4 %convolution_convert_fusion = bf16[28672,256]{1,0:T(8,128)(2,1)} fusion(bf16[28672,256]{1,0:T(8,128)(2,1)} %reshape.51, bf16[256,256]{1,0:T(8,128)(2,1)S(1)} %copy-done), kind=kOutput, calls=%fused_computation | convolution fusion | flops 3765436416 | bytes 29491200 | tf_op jit(solution)/shard_map/dot_general | solution.py:14
  45.6 0.0 copy-done.2
  45.6 10.5 %fusion = bf16[112,256,256]{1,2,0:T(8,128)(2,1)} fusion(f32[256,256]{0,1:T(8,128)S(1)} %add_divide_fusion, bf16[112,256,256]{2,1,0:T(8,128)(2,1)} %bitcast.27, bf16[256,256]{1,0:T(8,128)(2,1)S(1)} %copy-done.2), kind=kOutput, calls=%fused_computation.2 | convolution fusion | flops 3772776448 | bytes 29753344 | tf_op jit(solution)/shard_map/ai,naj->nij/dot_general | solution.py:18
  56.1 20.8 %copy.16 = bf16[14,8,256,256]{3,1,2,0:T(8,128)(2,1)} copy(bf16[14,8,256,256]{2,3,1,0:T(8,128)(2,1)} %bitcast.28) | data formatting | bytes 29360128
  76.8 65.8 %all-gather.2.cloned.1.call-done = bf16[128,65536]{1,0:T(8,128)(2,1)} async-done(((bf16[8,65536]{1,0:T(8,128)(2,1)}), bf16[128,65536]{1,0:T(8,128)(2,1)}) %all-gather.2.cloned.1.call-update) | async-done | bytes 16777232 | tf_op jit(solution)/shard_map/all_gather | solution.py:34
  142.7 0.0 copy-start.1
  142.7 13.0 %fusion.4 = (f32[128]{0:T(128)S(1)}, f32[112,128]{1,0:T(8,128)}) fusion(bf16[112,65536]{1,0:T(8,128)(2,1)} %bitcast.26, bf16[128,65536]{1,0:T(8,128)(2,1)} %all-gather.2.cloned.1.call-done), kind=kOutput, calls=%fused_computation.11 | convolution fusion | flops 1879076736 | bytes 31515136 | tf_op jit(solution)/shard_map/dot_general | solution.py:32
  155.6 30.6 %psum.7 = f32[128]{0:T(128)S(1)} all-reduce(f32[128]{0:T(128)S(1)} %get-tuple-element.2), channel_id=1, replica_groups=mesh['groups'=2,'blk'=16] {'blk'}, use_global_device_ids=true, to_apply=%region_1.0 | all-reduce | flops 128 | bytes 1024 | tf_op jit(solution)/shard_map/psum | solution.py:41
  186.3 0.6 dynamic-slice_multiply_fusion
  186.9 0.0 copy-done.1
Async XLA Ops:
  7.2 1.8 copy-start
  7.2 135.5 %all-gather.2.cloned.1.call-start = ((), (), s32[]{:S(2)}) async-start(), calls=%async_computation | async-start | bytes 17825792 | tf_op jit(solution)/shard_map/all_gather | solution.py:34
  12.9 18.1 %copy-start.3 = (f32[256]{0:T(256)S(1)}, f32[256]{0:T(256)}, u32[]{:S(2)}) copy-start(f32[256]{0:T(256)} %param.11) | copy-start | bytes 3076
  12.9 18.1 %copy-start.4 = (f32[256]{0:T(256)S(1)}, f32[256]{0:T(256)}, u32[]{:S(2)}) copy-start(f32[256]{0:T(256)} %param.10) | copy-start | bytes 3076
  31.1 14.5 %copy-start.2 = (bf16[256,256]{1,0:T(8,128)(2,1)S(1)}, bf16[256,256]{1,0:T(8,128)(2,1)}, u32[]{:S(2)}) copy-start(bf16[256,256]{1,0:T(8,128)(2,1)} %param.8) | copy-start | bytes 393220
  142.7 44.2 %copy-start.1 = (bf16[256,256]{1,0:T(8,128)(2,1)S(1)}, bf16[256,256]{1,0:T(8,128)(2,1)}, u32[]{:S(2)}) copy-start(bf16[256,256]{1,0:T(8,128)(2,1)} %param.9) | copy-start | bytes 393220
Sparse Core Ops, SparseCore 0:
  13.0 129.5 all-gather.1
where the time goes:
time: 195 us; the launch traced here: 194 us
  waiting for transfers between devices  65.8 us (34%)
  local copies, waits for them, and re-layouts  42.7 us (22%)
  matrix products  39.7 us (20%)
  blocking collectives  30.6 us (16%)
  between operations  14.1 us (7%)
    all_gather x1, waiting for transfers between devices, local(): lax.all_gather(train_eigen, 'blk', axis=0, tiled=True)  65.8 us
    psum x1, blocking collectives, local(): summed = lax.psum(column_terms, 'blk')  30.6 us
    unnamed x12, local copies, waits for them, and re-layouts  22.4 us
    reshape x2, local copies, waits for them, and re-layouts, rotate(): gradients.reshape(count * side, side)  19.8 us
    dot_general x2, matrix products, rotate(): jnp.dot(gradients.reshape(count * side, side), basis_in, preferred_elemen...  14.9 us
    dot_general x1, matrix products, local(): lax.dot_general(query_eigen, lax.all_gather(train_eigen, 'blk', axis=0, t...  13 us
    dot_general x2, matrix products, rotate(): jnp.einsum('ai,naj->nij', basis_out, half, preferred_element_type=jnp.flo...  11.9 us
  transfers between devices with their start and end apart: 1, of which 1 were waited for; matrix products, arithmetic and copies ran while one was open for 33% of the time, Pallas kernels for 0%

commit v1 on v0

v1 whole, which is shorter than its diff:
```python
import functools
import math

import jax
import jax.numpy as jnp
from jax import lax
from jax.experimental import pallas as pl
from jax.experimental.pallas import tpu as pltpu
from jax.sharding import PartitionSpec as P

damping = 0.1
F32, BF16 = jnp.float32, jnp.bfloat16
CORES = 2
LANES = 128
HALF_CHUNKS = 8
Y_FIRST = 1
NN = (((1,), (0,)), ((), ()))
NT = (((1,), (1,)), ((), ()))


def dot(a, b, dims=NN, precision=None):
    return lax.dot_general(a, b, dims, precision=precision, preferred_element_type=F32)


def split(x):
    high = x.astype(BF16)
    return high, (x - high.astype(F32)).astype(BF16)


def kernel(Z, Y, train_ref, bo_ref, bi_ref, eo_ref, ei_ref, q_ref, infl_ref, tot_ref,
           buf, flat, queries, sums, q_sem, first_send, first_recv, got, shared,
           up_send, down_send, y_send, core_send, sum_send, sum_recv):
    n = Z * Y * CORES
    NC = HALF_CHUNKS
    nyf = Y_FIRST if Y > 1 else 0
    trains, side = train_ref.shape[0], train_ref.shape[1]
    rows = q_ref.shape[0]
    tiles = buf.shape[0]
    pack = side // tiles
    per_half = tiles // 2
    per = per_half // NC

    me = lax.axis_index("blk")
    core = lax.rem(me, CORES)
    chip = lax.div(me, CORES)
    y = lax.rem(chip, Y)
    z = lax.div(chip, Y)
    mine, other = core, 1 - core
    partner = chip * CORES + (1 - core)
    y_chip = z * Y + (1 - y)

    q_copy = pltpu.make_async_copy(q_ref, queries, q_sem)
    q_copy.start()

    barrier = pltpu.get_barrier_semaphore()

    def greet(step, carry):
        pl.semaphore_signal(barrier, inc=1, device_id={"blk": lax.rem(me + step, n)},
                            device_id_type=pl.DeviceIdType.MESH)
        return carry
    lax.fori_loop(1, n, greet, 0)

    bo, bi = bo_ref[...], bi_ref[...]
    bot = bo.astype(F32).T.astype(BF16)
    bit = bi.astype(F32).T.astype(BF16)
    weights = 1.0 / (jnp.broadcast_to(eo_ref[...], (side, side)).T * ei_ref[...] + damping)
    for t in range(trains):
        hi, lo = split(dot(train_ref[t], bi))
        turned = dot(bot, hi) + dot(bot, lo)
        hi, lo = split(turned * weights)
        back = dot(hi, bit) + dot(lo, bit)
        hi, lo = split(back)
        vector = dot(bo, hi) + dot(bo, lo)
        for c in range(side // LANES):
            flat[c, pl.ds(t, side, stride=trains), :] = vector[:, c * LANES:(c + 1) * LANES]
    for c in range(side // LANES):
        buf[:, me, :, c * LANES:(c + 1) * LANES] = (
            flat[c].astype(BF16).reshape(tiles, pack * trains, LANES))

    pl.semaphore_wait(barrier, n - 1)

    def remote(src, send, recv, device):
        return pltpu.make_async_remote_copy(
            src_ref=src, dst_ref=src, send_sem=send, recv_sem=recv,
            device_id={"blk": device}, device_id_type=pl.DeviceIdType.MESH)

    def span(half, k):
        return pl.ds(half * per_half + k * per, per)

    def first(half, k):
        i = half * NC + k
        return remote(buf.at[span(half, k), me], first_send.at[i], first_recv.at[i], partner)

    def first_wait(half, k):
        i = half * NC + k
        remote(buf.at[span(half, k), partner], first_send.at[i], first_recv.at[i], partner).wait_recv()

    def piece(half, o, k):
        return buf.at[span(half, k), pl.ds(o * CORES, CORES)]

    def to_chip(o, k, sems, target):
        i = o * NC + k
        return remote(piece(mine, o, k), sems.at[i], got.at[i], target * CORES + core)

    def up(o, k):
        return to_chip(o, k, up_send, chip + Y)

    def down(o, k):
        return to_chip(o, k, down_send, chip - Y)

    def across(o, k):
        return to_chip(o, k, y_send, y_chip)

    def core_copy(o, k):
        i = o * NC + k
        return remote(piece(mine, o, k), core_send.at[i], shared.at[i], partner)

    def arrived(o, k):
        i = o * NC + k
        remote(piece(mine, o, k), up_send.at[i], got.at[i], partner).wait_recv()

    def core_arrived(o, k):
        i = o * NC + k
        remote(piece(other, o, k), core_send.at[i], shared.at[i], partner).wait_recv()

    def chunks(low, high, body):
        def step(k, carry):
            body(k)
            return carry
        if high > low:
            lax.fori_loop(low, high, step, 0)

    has_up, has_down = z + 1 < Z, z > 0

    def start_z(o, k):
        pl.when(has_up)(lambda: up(o, k).start())
        pl.when(has_down)(lambda: down(o, k).start())

    chunks(0, NC, lambda k: first(other, k).start())
    chunks(0, NC, lambda k: first(mine, k).start())

    def begin(k):
        first_wait(mine, k)
        start_z(chip, k)
        if Y > 1:
            across(chip, k).start()
    chunks(0, NC, begin)

    if Y > 1:
        def cross(k):
            arrived(y_chip, k)
            start_z(y_chip, k)
            core_copy(y_chip, k).start()
        chunks(0, nyf, cross)

    def from_y(o, k):
        arrived(o, k)
        core_copy(o, k).start()

    def side_step(d, sign, k):
        oz = z + sign * d
        inside = oz >= 0 if sign < 0 else oz < Z
        more = has_up if sign < 0 else has_down

        @pl.when(inside)
        def _():
            def forward(o):
                arrived(o, k)

                @pl.when(more)
                def _():
                    (up if sign < 0 else down)(o, k).start()
            o = oz * Y + y
            forward(o)
            if Y > 1:
                pl.when(k >= nyf)(lambda: across(o, k).start())
            core_copy(o, k).start()
            if nyf:
                @pl.when(k < nyf)
                def _():
                    far = oz * Y + (1 - y)
                    forward(far)
                    core_copy(far, k).start()

    def y_side(d, sign, k):
        oz = z + sign * d
        inside = oz >= 0 if sign < 0 else oz < Z
        pl.when(inside)(lambda: from_y(oz * Y + (1 - y), k))

    def plane(d, carry):
        def one(k):
            side_step(d, -1, k)
            side_step(d, 1, k)
            if Y > 1:
                @pl.when(k >= nyf)
                def _():
                    @pl.when(d == 1)
                    def _():
                        from_y(y_chip, k)

                    @pl.when(d > 1)
                    def _():
                        y_side(d - 1, -1, k)
                        y_side(d - 1, 1, k)
        chunks(0, NC, one)
        return carry
    lax.fori_loop(1, Z, plane, 0)

    width = n * pack * trains

    def score(half, k, acc):
        accs = list(acc)
        for i in range(per):
            tile = half * per_half + k * per + i
            block = buf[tile].reshape(width, side)
            for a in range(pack):
                col = pl.multiple_of((tile * pack + a) * side, side)
                accs[a] = accs[a] + dot(queries[:, pl.ds(col, side)], block, NT)
        return tuple(accs)

    def others_arrived(k):
        first_wait(other, k)

        def one(s, carry):
            core_arrived(lax.rem(chip + s, Z * Y), k)
            return carry
        lax.fori_loop(1, Z * Y, one, 0)

    q_copy.wait()

    def last(k, acc):
        if Y > 1:
            @pl.when(k >= nyf)
            def _():
                if Z == 1:
                    from_y(y_chip, k)
                else:
                    y_side(Z - 1, -1, k)
                    y_side(Z - 1, 1, k)
        return score(mine, k, acc)

    def rest(k, acc):
        others_arrived(k)
        return score(other, k, acc)

    acc = tuple(jnp.zeros((rows, width), F32) for _ in range(pack))
    acc = last(0, acc)

    def both(k, acc):
        return rest(k - 1, last(k, acc))
    acc = lax.fori_loop(1, NC, both, acc)
    acc = rest(NC - 1, acc)

    column = lax.broadcasted_iota(jnp.int32, (1, width), 1)
    which = lax.rem(lax.div(column, trains), pack)
    merged = acc[0]
    for a in range(1, pack):
        merged = jnp.where(which == a, acc[a], merged)
    source = lax.broadcasted_iota(jnp.int32, (width, n * trains), 0)
    place = lax.div(source, pack * trains) * trains + lax.rem(source, trains)
    target = lax.broadcasted_iota(jnp.int32, (width, n * trains), 1)
    pick = jnp.where(place == target, 1.0, 0.0).astype(F32)
    influence = dot(merged, pick, precision=lax.Precision.HIGHEST) / float(side)
    infl_ref[...] = influence

    sums[me] = jnp.broadcast_to(jnp.sum(influence, axis=0, keepdims=True), sums.shape[1:])

    def sum_copy(step):
        to = lax.rem(me + step, n)
        return remote(sums.at[me], sum_send.at[step], sum_recv.at[me], to)

    def sum_wait(step):
        src = lax.rem(me + step, n)
        remote(sums.at[src], sum_send.at[step], sum_recv.at[src], src).wait_recv()

    chunks(1, n, lambda s: sum_copy(s).start())

    chunks(0, NC, lambda k: first(other, k).wait_send())
    chunks(0, NC, lambda k: first(mine, k).wait_send())

    def own_left(o, k):
        pl.when(has_up)(lambda: up(o, k).wait_send())
        pl.when(has_down)(lambda: down(o, k).wait_send())

    def left(k):
        own_left(chip, k)
        if Y > 1:
            across(chip, k).wait_send()
            pl.when(k < nyf)(lambda: own_left(y_chip, k))
            core_copy(y_chip, k).wait_send()

        def one(oz, carry):
            near, far = oz * Y + y, oz * Y + (1 - y)

            @pl.when(oz != z)
            def _():
                core_copy(near, k).wait_send()
                pl.when((oz < z) & has_up)(lambda: up(near, k).wait_send())
                pl.when((oz > z) & has_down)(lambda: down(near, k).wait_send())
                if Y > 1:
                    core_copy(far, k).wait_send()
                    pl.when(k >= nyf)(lambda: across(near, k).wait_send())
                    pl.when((k < nyf) & (oz < z) & has_up)(lambda: up(far, k).wait_send())
                    pl.when((k < nyf) & (oz > z) & has_down)(lambda: down(far, k).wait_send())
            return carry
        lax.fori_loop(0, Z, one, 0)
    chunks(0, NC, left)

    chunks(1, n, sum_wait)
    total = jnp.sum(sums[...], axis=0)
    tot_ref[...] = total * (1.0 / math.sqrt(rows * n))
    chunks(1, n, lambda s: sum_copy(s).wait_send())


def grid_of(mesh):
    n = mesh.shape["blk"]
    chips = n // CORES
    try:
        group = mesh.devices.reshape(-1, n)[0]
        Y = len({tuple(d.coords[:2]) for d in group})
    except AttributeError:
        Y = 2 if chips % 2 == 0 else 1
    return chips // Y, Y


def local(Z, Y, query_grads, train_grads, basis_out, basis_in, eigen_out, eigen_in):
    side = basis_in.shape[0]
    trains = train_grads.shape[0]
    rows = query_grads.shape[0]
    n = Z * Y * CORES
    pack = 16 // trains
    tiles = side // pack
    pieces = Z * Y * HALF_CHUNKS
    dma = pltpu.SemaphoreType.DMA
    vmem = pl.BlockSpec(memory_space=pltpu.VMEM)
    influence, totals = pl.pallas_call(
        functools.partial(kernel, Z, Y),
        out_shape=(jax.ShapeDtypeStruct((rows, n * trains), F32),
                   jax.ShapeDtypeStruct((8, n * trains), F32)),
        in_specs=[vmem] * 5 + [pl.BlockSpec(memory_space=pl.ANY)],
        out_specs=(vmem, vmem),
        scratch_shapes=[
            pltpu.VMEM((tiles, n, pack * trains, side), BF16),
            pltpu.VMEM((side // LANES, side * trains, LANES), F32),
            pltpu.VMEM(query_grads.shape, BF16),
            pltpu.VMEM((n, 8, n * trains), F32),
            dma(()),
            dma((2 * HALF_CHUNKS,)), dma((2 * HALF_CHUNKS,)),
            dma((pieces,)), dma((pieces,)),
            dma((pieces,)), dma((pieces,)), dma((pieces,)), dma((pieces,)),
            dma((n,)), dma((n,)),
        ],
        compiler_params=pltpu.CompilerParams(
            collective_id=0, has_side_effects=True, vmem_limit_bytes=60 * 2**20),
        cost_estimate=pl.CostEstimate(
            flops=4 * rows * side * side * n * trains,
            bytes_accessed=2 * rows * side * side, transcendentals=0),
    )(train_grads.reshape(trains, side, side), basis_out, basis_in,
      eigen_out.reshape(1, side), eigen_in.reshape(1, side), query_grads)
    own = lax.dynamic_slice_in_dim(totals[0], lax.axis_index("blk") * trains, trains)
    return influence, own


def solution(mesh):
    Z, Y = grid_of(mesh)
    return jax.shard_map(
        functools.partial(local, Z, Y),
        mesh=mesh,
        in_specs=(P(("groups", "blk"), None), P(("groups", "blk"), None), P(), P(), P(), P()),
        out_specs=(P(("groups", "blk"), None), P(("groups", "blk"))),
        check_vma=False,
    )
```

time: 195 us -> 126 us (0.65)
  Pallas kernels: 0 us -> 120 us
  waiting for transfers between devices: 65.8 us -> 0 us
  matrix products: 39.7 us -> 0 us
  local copies, waits for them, and re-layouts: 42.7 us -> 5.14 us
  blocking collectives: 30.6 us -> 0 us
  between operations: 14.1 us -> 0.64 us
    pallas_call x0 -> x1, Pallas kernels: none -> 120 us  [local(): pl.pallas_call(functools.partial(kernel, Z, Y), out_shape=(jax.ShapeDtype...]
    all_gather x1 -> x0, waiting for transfers between devices: 65.8 us -> none  [local(): lax.all_gather(train_eigen, 'blk', axis=0, tiled=True)]
    dot_general x5 -> x0, matrix products: 39.7 us -> none  [the longest x2 14.9 us: rotate(): jnp.dot(gradients.reshape(count * side, side), basis_in, preferred_elemen...]
    psum x1 -> x0, blocking collectives: 30.6 us -> none  [local(): summed = lax.psum(column_terms, 'blk')]
    reshape x2 -> x0, local copies, waits for them, and re-layouts: 19.8 us -> none  [rotate(): gradients.reshape(count * side, side)]
    unnamed x12 -> x2, local copies, waits for them, and re-layouts: 22.4 us -> 3.86 us
  transfers between devices with their start and end apart: 1 -> 0, of which waited for: 1 -> 0; matrix products, arithmetic and copies ran while one was open for 33% -> 0% of each run, Pallas kernels for 0% -> 0%
where the time goes in v1:
time: 126 us; the launch traced here: 125 us
  Pallas kernels  120 us (95%)
  local copies, waits for them, and re-layouts  5.14 us (4%)
    pallas_call x1, Pallas kernels, local(): pl.pallas_call(functools.partial(kernel, Z, Y), out_shape=(jax.ShapeDtype...  120 us
    unnamed x2, local copies, waits for them, and re-layouts  3.86 us

profile of v1, /device:TPU:0, one launch (start us, length us, event | category | flops | bytes accessed | tf_op | source)
XLA Modules:
  0.0 125.4 jit_solution(6872175008616946310)
XLA Ops:
  0.6 2.4 %copy.10 = bf16[1,8,256,256]{3,2,1,0:T(8,128)(2,1)} copy(bf16[1,8,256,256]{3,1,2,0:T(8,128)(2,1)} %bitcast.9) | data formatting | bytes 2097152
  3.0 119.6 %shard_map.77 = (f32[112,128]{1,0:T(8,128)}, f32[8,128]{1,0:T(8,128)}) custom-call(bf16[8,256,256]{2,1,0:T(8,128)(2,1)} %bitcast.8, bf16[256,256]{1,0:T(8,128)(2,1)} %bo_ref.1, bf16[256,256]{1,0:T(8,128)(2,1)} %bi_ref.1, f32[1,256]{1,0:T(1,128)} %bitcast.10, f32[1,256]{1,0:T(1,128)} %bitcast.11, bf16[112,65536]{1,0:T(8,128)(2,1)} %q_ref.1), custom_call_target="tpu_custom_call" | custom-call | flops 3758096384 | bytes 14680064 | tf_op jit(solution)/shard_map/pallas_call | solution.py:336
  122.7 0.7 slice.3
  123.4 0.6 dynamic-slice_bitcast_fusion
  124.0 1.4 %copy.12 = f32[112,128]{1,0:T(8,128)} copy(f32[112,128]{1,0:T(8,128)} %get-tuple-element.8) | data formatting | bytes 114688

commit v2 on v1

--- a/solution.py
+++ b/solution.py
@@ -33,7 +33,7 @@
     n = Z * Y * CORES
     NC = HALF_CHUNKS
     nyf = Y_FIRST if Y > 1 else 0
-    trains, side = train_ref.shape[0], train_ref.shape[1]
+    trains, side = train_ref.shape[0], bo_ref.shape[0]
     rows = q_ref.shape[0]
     tiles = buf.shape[0]
     pack = side // tiles
@@ -64,8 +64,14 @@
     bot = bo.astype(F32).T.astype(BF16)
     bit = bi.astype(F32).T.astype(BF16)
     weights = 1.0 / (jnp.broadcast_to(eo_ref[...], (side, side)).T * ei_ref[...] + damping)
+    halves = range(side // LANES)
+    for a in range(side):
+        for c in halves:
+            flat[c, a * trains:(a + 1) * trains, :] = (
+                train_ref[:, a * side + c * LANES:a * side + (c + 1) * LANES].astype(F32))
     for t in range(trains):
-        hi, lo = split(dot(train_ref[t], bi))
+        matrix = jnp.concatenate([flat[c, pl.ds(t, side, stride=trains), :] for c in halves], axis=1)
+        hi, lo = split(dot(matrix.astype(BF16), bi))
         turned = dot(bot, hi) + dot(bot, lo)
         hi, lo = split(turned * weights)
         back = dot(hi, bit) + dot(lo, bit)
@@ -139,70 +145,60 @@
     chunks(0, NC, lambda k: first(other, k).start())
     chunks(0, NC, lambda k: first(mine, k).start())
 
+    near = NC - nyf
+
+    def cross_first(k):
+        first_wait(mine, k)
+        across(chip, k).start()
+    chunks(near, NC, cross_first)
+
     def begin(k):
         first_wait(mine, k)
         start_z(chip, k)
         if Y > 1:
             across(chip, k).start()
-    chunks(0, NC, begin)
-
-    if Y > 1:
-        def cross(k):
-            arrived(y_chip, k)
-            start_z(y_chip, k)
-            core_copy(y_chip, k).start()
-        chunks(0, nyf, cross)
+    chunks(0, near, begin)
+    chunks(near, NC, lambda k: start_z(chip, k))
+
+    def cross(k):
+        arrived(y_chip, k)
+        start_z(y_chip, k)
+        core_copy(y_chip, k).start()
+    chunks(near, NC, cross)
 
     def from_y(o, k):
         arrived(o, k)
         core_copy(o, k).start()
 
-    def side_step(d, sign, k):
-        oz = z + sign * d
-        inside = oz >= 0 if sign < 0 else oz < Z
-        more = has_up if sign < 0 else has_down
-
-        @pl.when(inside)
+    def pass_on(d, k, column, to_y):
+        def one(oz, inside, more, onward):
+            @pl.when(inside)
+            def _():
+                o = oz * Y + column
+                arrived(o, k)
+                pl.when(more)(lambda: onward(o, k).start())
+                if to_y:
+                    across(o, k).start()
+                core_copy(o, k).start()
+        one(z - d, z - d >= 0, has_up, up)
+        one(z + d, z + d < Z, has_down, down)
+
+    def y_pieces(d, k):
+        @pl.when(d == 0)
         def _():
-            def forward(o):
-                arrived(o, k)
-
-                @pl.when(more)
-                def _():
-                    (up if sign < 0 else down)(o, k).start()
-            o = oz * Y + y
-            forward(o)
-            if Y > 1:
-                pl.when(k >= nyf)(lambda: across(o, k).start())
-            core_copy(o, k).start()
-            if nyf:
-                @pl.when(k < nyf)
-                def _():
-                    far = oz * Y + (1 - y)
-                    forward(far)
-                    core_copy(far, k).start()
-
-    def y_side(d, sign, k):
-        oz = z + sign * d
-        inside = oz >= 0 if sign < 0 else oz < Z
-        pl.when(inside)(lambda: from_y(oz * Y + (1 - y), k))
+            from_y(y_chip, k)
+
+        @pl.when(d > 0)
+        def _():
+            pl.when(z - d >= 0)(lambda: from_y((z - d) * Y + (1 - y), k))
+            pl.when(z + d < Z)(lambda: from_y((z + d) * Y + (1 - y), k))
 
     def plane(d, carry):
-        def one(k):
-            side_step(d, -1, k)
-            side_step(d, 1, k)
-            if Y > 1:
-                @pl.when(k >= nyf)
-                def _():
-                    @pl.when(d == 1)
-                    def _():
-                        from_y(y_chip, k)
-
-                    @pl.when(d > 1)
-                    def _():
-                        y_side(d - 1, -1, k)
-                        y_side(d - 1, 1, k)
-        chunks(0, NC, one)
+        chunks(0, near, lambda k: pass_on(d, k, y, Y > 1))
+        chunks(near, NC, lambda k: pass_on(d, k, y, False))
+        chunks(near, NC, lambda k: pass_on(d, k, 1 - y, False))
+        if Y > 1:
+            chunks(0, near, lambda k: y_pieces(d - 1, k))
         return carry
     lax.fori_loop(1, Z, plane, 0)
 
@@ -230,13 +226,7 @@
 
     def last(k, acc):
         if Y > 1:
-            @pl.when(k >= nyf)
-            def _():
-                if Z == 1:
-                    from_y(y_chip, k)
-                else:
-                    y_side(Z - 1, -1, k)
-                    y_side(Z - 1, 1, k)
+            pl.when(k < near)(lambda: y_pieces(Z - 1, k))
         return score(mine, k, acc)
 
     def rest(k, acc):
@@ -286,22 +276,22 @@
         own_left(chip, k)
         if Y > 1:
             across(chip, k).wait_send()
-            pl.when(k < nyf)(lambda: own_left(y_chip, k))
+            pl.when(k >= near)(lambda: own_left(y_chip, k))
             core_copy(y_chip, k).wait_send()
 
         def one(oz, carry):
-            near, far = oz * Y + y, oz * Y + (1 - y)
+            same, far = oz * Y + y, oz * Y + (1 - y)
 
             @pl.when(oz != z)
             def _():
-                core_copy(near, k).wait_send()
-                pl.when((oz < z) & has_up)(lambda: up(near, k).wait_send())
-                pl.when((oz > z) & has_down)(lambda: down(near, k).wait_send())
+                core_copy(same, k).wait_send()
+                pl.when((oz < z) & has_up)(lambda: up(same, k).wait_send())
+                pl.when((oz > z) & has_down)(lambda: down(same, k).wait_send())
                 if Y > 1:
                     core_copy(far, k).wait_send()
-                    pl.when(k >= nyf)(lambda: across(near, k).wait_send())
-                    pl.when((k < nyf) & (oz < z) & has_up)(lambda: up(far, k).wait_send())
-                    pl.when((k < nyf) & (oz > z) & has_down)(lambda: down(far, k).wait_send())
+                    pl.when(k < near)(lambda: across(same, k).wait_send())
+                    pl.when((k >= near) & (oz < z) & has_up)(lambda: up(far, k).wait_send())
+                    pl.when((k >= near) & (oz > z) & has_down)(lambda: down(far, k).wait_send())
             return carry
         lax.fori_loop(0, Z, one, 0)
     chunks(0, NC, left)
@@ -355,7 +345,7 @@
         cost_estimate=pl.CostEstimate(
             flops=4 * rows * side * side * n * trains,
             bytes_accessed=2 * rows * side * side, transcendentals=0),
-    )(train_grads.reshape(trains, side, side), basis_out, basis_in,
+    )(train_grads, basis_out, basis_in,
       eigen_out.reshape(1, side), eigen_in.reshape(1, side), query_grads)
     own = lax.dynamic_slice_in_dim(totals[0], lax.axis_index("blk") * trains, trains)
     return influence, own

time: 126 us -> 119 us (0.944)
  Pallas kernels: 120 us -> 115 us
  local copies, waits for them, and re-layouts: 5.14 us -> 2.71 us
    pallas_call x1, Pallas kernels: 120 us -> 115 us  [local(): pl.pallas_call(functools.partial(kernel, Z, Y), out_shape=(jax.ShapeDtype...]
    unnamed x2 -> x1, local copies, waits for them, and re-layouts: 3.86 us -> 1.44 us
where the time goes in v2:
time: 119 us; the launch traced here: 118 us
  Pallas kernels  115 us (97%)
  local copies, waits for them, and re-layouts  2.71 us (2%)
    pallas_call x1, Pallas kernels, local(): pl.pallas_call(functools.partial(kernel, Z, Y), out_shape=(jax.ShapeDtype...  115 us

profile of v2, /device:TPU:0, one launch (start us, length us, event | category | flops | bytes accessed | tf_op | source)
XLA Modules:
  0.0 118.4 jit_solution(1836420427956819566)
XLA Ops:
  0.6 115.0 %shard_map.77 = (f32[112,128]{1,0:T(8,128)}, f32[8,128]{1,0:T(8,128)}) custom-call(bf16[8,65536]{1,0:T(8,128)(2,1)} %train_ref.1, bf16[256,256]{1,0:T(8,128)(2,1)} %bo_ref.1, bf16[256,256]{1,0:T(8,128)(2,1)} %bi_ref.1, f32[1,256]{1,0:T(1,128)} %bitcast.4, f32[1,256]{1,0:T(1,128)} %bitcast.5, bf16[112,65536]{1,0:T(8,128)(2,1)} %q_ref.1), custom_call_target="tpu_custom_call" | custom-call | flops 3758096384 | bytes 14680064 | tf_op jit(solution)/shard_map/pallas_call | solution.py:326
  115.7 0.7 slice.3
  116.4 0.6 dynamic-slice_bitcast_fusion
  117.0 1.4 %copy.9 = f32[112,128]{1,0:T(8,128)} copy(f32[112,128]{1,0:T(8,128)} %get-tuple-element.8) | data formatting | bytes 114688
